TPU v7x, 32 devices: a whole 2x2x4 slice. The times are simulated.
32 devices in a mesh: lists: 8 (over z, x), help: 4 (over y, core).
Axes of the slice: x: 2, y: 2, z: 4, core: 2. Of those that a mesh axis runs over, the one named last changes fastest.
Arguments:
- vectors: float32 [16, 1024, 768], P('lists', 'help'), may hold values from -6 to 6
- labels: int32 [16, 1024], P('lists', 'help'), may hold values from 0 to 1, as said below
- list_sizes: int32 [16], P('lists'), may hold values from 64 to 1024, as said below
- centroids: float32 [16, 768], P('lists'), may hold values from -4 to 4
- split_ids: int32 [4], replicated, may hold values from 0 to 15, as said below
- nearby: int32 [4, 8], replicated, may hold values from 0 to 15, as said below
- owner_map: int32 [16], replicated, may hold values from 0 to 15, as said below
- mover_source: int32 [4096], P(('lists', 'help')), may hold values from 0 to 511, as said below
- mover_dest: int32 [4096], P(('lists', 'help')), may hold values from -1 to 15, as said below
Outputs:
- gains: float32 [16, 1024], P('lists', 'help')
- arrivals: float32 [16, 512, 768], P('lists')
Inputs may be any that keep to these rules, and one draw needn't show every extreme that they name: `split_ids`: distinct list ids. `nearby`: for each split, 8 distinct list ids, none equal to the split list. `owner_map`: a permutation of the slots. `list_sizes`: every list has at least two live rows; every split list has at least 576 live rows; the first slot of every index of lists that does not hold a split list holds at least 832 live rows. `labels`: row 0 of every list has label 0 and row 1 label 1. `mover_source`: distinct rows of the source device's block, live ones first. `mover_dest`: -1 exactly where the mover's source row is not live; from one device at most 32 live movers go to lists stored on one index of lists; every list slot receives at most 512 rows in all. Numbers of movers counted from these ids (per device and slot, or running totals of them) are small exact integers and may cross devices in any exact integer encoding, several to a word.
All inputs are finite; a program needn't handle non-finite values.
Results may differ from a plain program's by a relative error of at most 0.0003.
Values sent between devices are 32-bit elements; how exact they have to be, the bound alone decides.
A program may use at most 64 MiB of HBM per device.

v0:
```python
import jax
import jax.numpy as jnp
from jax import lax
from jax.sharding import PartitionSpec as P

HIGH = lax.Precision.HIGHEST


def carried_in(part, axis, combine, identity):
    place = lax.axis_index(axis)
    gathered = lax.all_gather(part, axis)
    state = jnp.zeros_like(part) + jnp.asarray(identity, part.dtype)

    def one(hop, state):
        return combine(state, lax.dynamic_index_in_dim(gathered, hop, 0, False))

    return lax.fori_loop(0, place, one, state)


def add_counts(earlier, later):
    return earlier + later


def place_rows(rows_in, codes_in, slots_total, width):
    where_to = jnp.where(codes_in >= 0.0, codes_in, float(slots_total)).astype(jnp.int32)
    return jnp.zeros((slots_total, width), jnp.float32).at[where_to].set(rows_in, mode="drop")


def local(
    vectors, labels, list_sizes, centroids, split_ids, nearby, owner_map, mover_source, mover_dest
):
    list_dev, rows, width = vectors.shape
    lists_count = lax.axis_size("lists")
    help_count = lax.axis_size("help")
    first = lax.axis_index("lists") * list_dev
    start_row = lax.axis_index("help") * rows
    local_slots = first + jnp.arange(list_dev, dtype=jnp.int32)
    row_index = start_row + jnp.arange(rows, dtype=jnp.int32)
    valid = row_index[None, :] < list_sizes[:, None]
    halves = jnp.stack([(labels == 0) & valid, (labels == 1) & valid], axis=1).astype(jnp.float32)
    partial_value = jnp.einsum("kar,krd->kad", halves, vectors, precision=HIGH)
    counts = jnp.sum(halves, axis=2)
    split_slots = owner_map[split_ids]
    select = (split_slots[:, None] == local_slots[None, :]).astype(jnp.float32)
    sums, totals = lax.psum(
        (
            jnp.einsum("sk,kad->sad", select, partial_value, precision=HIGH),
            jnp.einsum("sk,ka->sa", select, counts, precision=HIGH),
        ),
        ("lists", "help"),
    )
    new_cent = sums / totals[:, :, None]
    cents = new_cent.reshape(-1, width)
    sq_cent = jnp.sum(cents * cents, axis=1)
    near_slots = owner_map[nearby]
    hit = jnp.any(near_slots[None, :, :] == local_slots[:, None, None], axis=2)
    paired = jnp.repeat(hit, 2, axis=1)
    square = jnp.sum(vectors * vectors, axis=2)
    cross = jnp.einsum("krd,cd->krc", vectors, cents, precision=HIGH)
    dist = square[:, :, None] - 2.0 * cross + sq_cent[None, None, :]
    far = jnp.min(jnp.where(paired[:, None, :], dist, 1e30), axis=2)
    own_cross = jnp.einsum("krd,kd->kr", vectors, centroids, precision=HIGH)
    own = square - 2.0 * own_cross + jnp.sum(centroids * centroids, axis=1)[:, None]
    touched = valid & jnp.any(hit, axis=1)[:, None]
    gains = jnp.where(touched, (own - far) / width, 0.0)
    moves = mover_source.shape[0]
    depth = max(2, (moves + lists_count - 1) // lists_count * 2)
    arrive_cap = lists_count * help_count * ((depth + list_dev - 1) // list_dev)
    total_lists = list_dev * lists_count
    flat_rows = vectors.reshape(list_dev * rows, width)
    moving = flat_rows[mover_source]
    live_move = mover_dest >= 0
    dest_slot = jnp.where(live_move, owner_map[jnp.maximum(mover_dest, 0)], total_lists)
    slot_hit = (dest_slot[:, None] == jnp.arange(total_lists, dtype=jnp.int32)[None, :]).astype(
        jnp.int32
    )
    before = jnp.cumsum(slot_hit, axis=0) - slot_hit
    sent_counts = jnp.sum(slot_hit, axis=0)
    offsets = carried_in(sent_counts, ("lists", "help"), add_counts, jnp.zeros_like(sent_counts))
    position = jnp.sum((before + offsets[None, :]) * slot_hit, axis=1)
    dest_dev = dest_slot // list_dev
    dest_local = dest_slot % list_dev
    peers = (dest_dev[:, None] == jnp.arange(lists_count, dtype=jnp.int32)[None, :]).astype(
        jnp.int32
    )
    ranking = jnp.sum(jnp.cumsum(peers, axis=0) * peers, axis=1) - 1
    bucket_at = jnp.where(live_move, dest_dev * depth + ranking, lists_count * depth)
    buckets = (
        jnp.zeros((lists_count * depth, width), jnp.float32).at[bucket_at].set(moving, mode="drop")
    )
    place_code = (dest_local * arrive_cap + position).astype(jnp.float32)
    codes = (
        jnp.full((lists_count * depth,), -1.0, jnp.float32)
        .at[bucket_at]
        .set(place_code, mode="drop")
    )
    landed, landed_codes = (
        lax.all_to_all(
            buckets.reshape(lists_count, depth, width),
            "lists",
            split_axis=0,
            concat_axis=0,
            tiled=True,
        ),
        lax.all_to_all(
            codes.reshape(lists_count, depth), "lists", split_axis=0, concat_axis=0, tiled=True
        ),
    )
    slots_total = list_dev * arrive_cap
    rows_all, codes_all = (
        lax.all_gather(landed.reshape(-1, width), "help", axis=0, tiled=True),
        lax.all_gather(landed_codes.reshape(-1), "help", axis=0, tiled=True),
    )
    arrived = place_rows(rows_all, codes_all, slots_total, width)
    return (gains, arrived.reshape(list_dev, arrive_cap, width))


def solution(mesh):
    in_specs = (
        P("lists", "help", None),
        P("lists", "help"),
        P("lists"),
        P("lists", None),
        P(),
        P(),
        P(),
        P(("lists", "help")),
        P(("lists", "help")),
    )
    out_specs = (P("lists", "help"), P("lists", None, None))
    return jax.shard_map(local, mesh=mesh, in_specs=in_specs, out_specs=out_specs, check_vma=False)
```

profile of v0, /device:TPU:0, one launch (start us, length us, event | category | flops | bytes accessed | tf_op | source)
XLA Modules:
  0.0 167.4 jit_solution(15964190058194931429)
XLA Ops:
  7.2 1.9 %fusion.36 = (s32[1]{0:T(128)}, s32[1]{0:T(128)}, s32[1]{0:T(128)}, s32[1]{0:T(128)}, s32[1]{0:T(128)}, /*index=5*/s32[1]{0:T(128)}, s32[1]{0:T(128)}, s32[1]{0:...) fusion(s32[16]{0:T(128)} %param.17), kind=kLoop, calls=%fused_computation.94 | loop fusion | bytes 128 | tf_op jit(solution)/shard_map/gather | solution.py:73
  9.2 10.7 %and_select_fusion.1 = (s32[128]{0:T(128)S(1)}, s32[128]{0:T(128)S(1)}) fusion(s32[]{:T(128)} %bitcast.22, s32[]{:T(128)} %bitcast.21, s32[]{:T(128)} %bitcast.20, s32[]{:T(128)} %bitcast.19, s32[]{:T(128)} %bitcast.18, s32[]{:T(128)} %bitcast.17, s32[]{:T(128)} %bitcast.16, s32[]{:T(128)} %bitcast.15, s32[]{:T(128)} %bitcast.14, s32[]{:T(128)} %bitcast.13, ...), kind=kLoop, calls=%fused_computation.77 | loop fusion | flops 6144 | bytes 1600 | tf_op jit(solution)/shard_map/jit(floor_divide)/jit(_where)/select_n | solution.py:81
  20.1 0.2 reduce_window_sum.23
  20.2 0.2 dynamic-update-slice
  20.5 42.0 %all-reduce = s32[512]{0:T(512)S(1)} all-reduce(s32[512]{0:T(512)S(1)} %dynamic-update-slice), channel_id=2, replica_groups=mesh['lists'=8,'help'=4] {'lists','help'}, use_global_device_ids=true, to_apply=%add | all-reduce | flops 512 | bytes 4096
  62.7 0.2 reduce_window_sum.22
  62.8 0.2 select_reduce_fusion.1
  63.0 0.7 compare_select_fusion.3
  63.7 0.2 select_reduce_fusion
  63.9 0.7 compare_select_fusion.4
  64.6 2.8 %scatter_custom_fusion.1 = f32[256,768]{1,0:T(8,128)S(1)} fusion(s32[128]{0:T(128)S(1)} %get-tuple-element.62, f32[512,768]{1,0:T(8,128)} %bitcast.57, s32[1024]{0:T(1024)S(1)} %pad_clamp_fusion, f32[]{:T(128)} %constant.47.clone.1), kind=kCustom, calls=%fused_computation.16 | custom fusion | bytes 786944 | tf_op jit(solution)/shard_map/scatter | solution.py:89
  67.4 24.8 %all_to_all.14 = f32[8,32,768]{2,1,0:T(8,128)} all-to-all(f32[8,32,768]{2,1,0:T(8,128)S(1)} %bitcast.59), channel_id=1, replica_groups=mesh['lists'=8,'help'=4] {'lists'}, dimensions={0} | all-to-all | bytes 1572864 | tf_op jit(solution)/shard_map/all_to_all | solution.py:98
  92.3 1.0 scatter_custom_fusion
  93.3 0.7 all_to_all.9
  93.9 3.6 %all-to-all-start = ((f32[8,1,32]{2,1,0:T(1,128)}), f32[8,1,32]{2,1,0:T(1,128)S(1)}, u32[]{:S(2)}, u32[]{:S(2)}) async-start(f32[8,1,32]{2,1,0:T(1,128)} %all_to_all.9), calls=%async_computation | async-start | bytes 8192 | tf_op jit(solution)/shard_map/all_to_all | solution.py:105
  97.7 0.6 gather_fusion.1
  98.4 0.2 fusion.21
  98.6 0.6 fusion.37
  99.3 0.3 fusion.13
  99.6 41.4 %all-reduce.1 = (f32[4,2,768]{2,0,1:T(4,128)S(1)}, f32[4,2]{0,1:T(2,128)S(1)}) all-reduce(f32[4,2,768]{2,0,1:T(4,128)S(1)} %fusion.13, f32[4,2]{0,1:T(2,128)S(1)} %fusion.21), channel_id=1, replica_groups=mesh['lists'=8,'help'=4] {'lists','help'}, use_global_device_ids=true, to_apply=%region_4.0 | all-reduce | flops 6152 | bytes 49216 | tf_op jit(solution)/shard_map/psum | solution.py:45
  140.9 0.2 multiply_reduce_fusion.1
  141.4 0.7 gather_fusion
  142.2 0.3 compare_reduce_fusion.1
  142.7 0.1 multiply_reduce_fusion.2
  142.8 0.2 multiply_reduce_fusion
  143.0 1.4 fusion.6
  144.4 1.4 fusion.15
  145.8 0.7 fusion.18
  146.5 0.5 broadcast.185
  147.0 0.7 reduce.5
  147.7 5.3 %all-gather.1 = f32[4,1,256]{2,1,0:T(1,128)S(1)} all-gather(f32[1,1,256]{2,1,0:T(1,128)S(1)} %reshape.141), channel_id=1, replica_groups=mesh['lists'=8,'help'=4] {'help'}, dimensions={0}, use_global_device_ids=true | all-gather | bytes 5120 | tf_op jit(solution)/shard_map/all_gather | solution.py:112
  153.1 7.5 %scatter_custom_fusion.2 = f32[1024,768]{1,0:T(8,128)} fusion(s32[1024]{0:T(1024)S(1)} %compare_select_fusion, f32[1024,768]{1,0:T(8,128)} %all-gather.4.cloned.1.call-done, f32[]{:T(128)} %constant.47.clone.1), kind=kCustom, calls=%fused_computation.7 | custom fusion | bytes 3146240 | tf_op jit(solution)/shard_map/scatter | solution.py:26
  (46 shorter events, 1.3 us)
Async XLA Ops:
  7.2 145.9 %all-gather.4.cloned.1.call-start = ((), (), s32[]{:S(2)}) async-start(), calls=%async_computation.2 | async-start | bytes 3932160 | tf_op jit(solution)/shard_map/all_gather | solution.py:111
  64.5 33.0 %copy-start.4 = (s32[2,256]{1,0:T(2,128)S(1)}, s32[2,256]{1,0:T(2,128)}, u32[]{:S(2)}) copy-start(s32[2,256]{1,0:T(2,128)} %param.12) | copy-start | bytes 6148
  64.5 33.0 %copy-start.5 = (s32[2]{0:T(128)S(1)}, s32[2]{0:T(128)}, u32[]{:S(2)}) copy-start(s32[2]{0:T(128)} %param.13) | copy-start | bytes 28
  64.6 33.1 %copy-start.6 = (s32[4]{0:T(128)S(1)}, s32[4]{0:T(128)}, u32[]{:S(2)}) copy-start(s32[4]{0:T(128)} %param.15) | copy-start | bytes 52
  64.6 33.1 %copy-start = (s32[16]{0:T(128)S(1)}, s32[16]{0:T(128)}, u32[]{:S(2)}) copy-start(s32[16]{0:T(128)} %param.17) | copy-start | bytes 196
  67.4 31.2 %copy-start.1 = (f32[2,256,768]{2,1,0:T(8,128)S(1)}, f32[2,256,768]{2,1,0:T(8,128)}, u32[]{:S(2)}) copy-start(f32[2,256,768]{2,1,0:T(8,128)} %param.11) | copy-start | bytes 4718596
  92.3 49.1 %copy-start.3 = (s32[4,8]{1,0:T(4,128)S(1)}, s32[4,8]{1,0:T(4,128)}, u32[]{:S(2)}) copy-start(s32[4,8]{1,0:T(4,128)} %param.16) | copy-start | bytes 388
  93.9 52.6 %all-to-all-start = ((f32[8,1,32]{2,1,0:T(1,128)}), f32[8,1,32]{2,1,0:T(1,128)S(1)}, u32[]{:S(2)}, u32[]{:S(2)}) async-start(f32[8,1,32]{2,1,0:T(1,128)} %all_to_all.9), calls=%async_computation | async-start | bytes 8192 | tf_op jit(solution)/shard_map/all_to_all | solution.py:105
  99.3 43.4 %copy-start.2 = (f32[2,768]{1,0:T(2,128)S(1)}, f32[2,768]{1,0:T(2,128)}, u32[]{:S(2)}) copy-start(f32[2,768]{1,0:T(2,128)} %param.14) | copy-start | bytes 18436
Sparse Core Ops, SparseCore 0:
  92.4 28.3 all-gather.3
where the time goes:
time: 168 us; the launch traced here: 167 us
  blocking collectives  114 us (68%)
  local copies, waits for them, and re-layouts  16.7 us (10%)
  other arithmetic  15.3 us (9%)
  between operations  14.2 us (8%)
  matrix products  3.97 us (2%)
  starting transfers between devices  3.63 us (2%)
    unnamed x1, blocking collectives  42 us
    psum x1, blocking collectives, local(): lax.psum((jnp.einsum('sk,kad->sad', select, partial_value, precision=HIGH...  41.4 us
    all_to_all x1, blocking collectives, local(): lax.all_to_all(buckets.reshape(lists_count, depth, width), 'lists', split...  24.8 us
    select_n x1, other arithmetic, local(): dest_dev = dest_slot // list_dev  10.7 us
    scatter x1, local copies, waits for them, and re-layouts, place_rows(): jnp.zeros((slots_total, width), jnp.float32).at[where_to]  7.46 us
    all_gather x1, blocking collectives, local(): lax.all_gather(landed_codes.reshape(-1), 'help', axis=0, tiled=True)  5.32 us
    all_to_all x1, starting transfers between devices, local(): lax.all_to_all(codes.reshape(lists_count, depth), 'lists', split_axis=0,...  3.59 us
  transfers between devices with their start and end apart: 2, of which 0 were waited for; matrix products, arithmetic and copies ran while one was open for 6% of the time, Pallas kernels for 0%

commit v1 on v0

v1 whole, which is shorter than its diff:
```python
import functools

import jax
import jax.numpy as jnp
from jax import lax
from jax.experimental import pallas as pl
from jax.experimental.pallas import tpu as pltpu
from jax.sharding import PartitionSpec as P

MESH = pl.DeviceIdType.MESH
F32 = jnp.float32
BF16 = jnp.bfloat16


def split_parts(x):
    hi = x.astype(BF16)
    return hi, (x - hi.astype(F32)).astype(BF16)


def dot(a, b):
    return lax.dot_general(a, b, (((1,), (0,)), ((), ())), preferred_element_type=F32)


def dot_t(a, b):
    return lax.dot_general(a, b, (((1,), (1,)), ((), ())), preferred_element_type=F32)


def iota(shape, axis):
    return lax.broadcasted_iota(jnp.int32, shape, axis)


def kernel(
    lists, helps, depth, cap, crows,
    vec, labels, cent, msrc, mdst, sizes, split_ids, nearby, owner,
    gains, out,
    vhi, vlo, buckets, recv, flag_out, flags, flag_mat, codes, parts, cents, table,
    s_flag, r_flag, s_fgat, r_fgat, s_bkt, r_bkt, s_core, r_core, s_y, r_y, s_rel, r_rel,
    s_part, r_part, s_cent, r_cent,
):
    me = lax.axis_index("lists")
    hp = lax.axis_index("help")
    list_dev, rows, width = vec.shape
    n_rows = list_dev * rows
    moves = mdst.shape[1]
    n_splits, near = nearby.shape
    total_lists = owner.shape[0]
    first = me * list_dev
    core = lax.rem(hp, 2) * -2 + 1 + hp
    far = lax.rem(hp + 2, 4)
    diag = lax.rem(core + 2, 4)

    barrier = pltpu.get_barrier_semaphore()

    def greet(d, c):
        pl.semaphore_signal(
            barrier, inc=1, device_id=(lax.rem(me + d, lists), hp), device_id_type=MESH
        )
        return c

    lax.fori_loop(1, lists, greet, 0)
    for d in range(1, helps):
        pl.semaphore_signal(
            barrier, inc=1, device_id=(me, lax.rem(hp + d, helps)), device_id_type=MESH
        )

    hi, lo = split_parts(vec[...].reshape(n_rows, width))
    vhi[...] = hi
    vlo[...] = lo

    lane = iota((crows, n_rows), 1)
    row = iota((crows, n_rows), 0)
    label = jnp.concatenate([labels[k : k + 1, :] for k in range(list_dev)], axis=1)
    limit = jnp.zeros((1, n_rows), jnp.int32)
    lane1 = iota((1, n_rows), 1)
    for k in range(list_dev):
        inside = (lane1 >= k * rows) & (lane1 < (k + 1) * rows)
        limit = jnp.where(inside, sizes[k] + k * rows - hp * rows, limit)
    live_label = jnp.where(lane1 < limit, label, -1)
    half = jnp.zeros((crows, n_rows), F32)
    for k in range(list_dev):
        for a in range(2):
            pick = (row == 2 * k + a) & (lane >= k * rows) & (lane < (k + 1) * rows)
            half = jnp.where(pick & (live_label == a), 1.0, half)
    hb = half.astype(BF16)
    mine = dot(hb, hi) + dot(hb, lo)
    number = jnp.sum(half, axis=1, keepdims=True)
    parts[hp, :, 0:width] = mine
    parts[hp, :, width:] = jnp.broadcast_to(number, (crows, 128))

    dest = mdst[...]
    slot = jnp.full((1, moves), -1, jnp.int32)
    for x in range(total_lists):
        slot = jnp.where(dest == x, owner[x], slot)
    alive = slot >= 0
    slot_f = slot.astype(F32)
    peer = jnp.where(alive, jnp.floor(slot_f / list_dev), -1.0)
    local = jnp.where(alive, slot_f - peer * list_dev + 1.0, 0.0)
    peer_is = peer == iota((lists, moves), 0).astype(F32)
    peers = jnp.where(peer_is, 1.0, 0.0)
    upper = jnp.where(iota((moves, moves), 0) < iota((moves, moves), 1), 1.0, 0.0).astype(BF16)
    rank = jnp.sum(dot(peers.astype(BF16), upper) * peers, axis=0, keepdims=True)
    at = jnp.where(alive, peer * depth + rank, -1.0).astype(jnp.int32)
    chosen = jnp.where(at == iota((lists * depth, moves), 0), 1.0, 0.0).astype(BF16)
    source = jnp.where(msrc[...] == iota((n_rows, moves), 0), 1.0, 0.0).astype(BF16)
    gather = dot_t(chosen, source).astype(BF16)
    buckets[...] = (dot(gather, hi) + dot(gather, lo)).reshape(lists, depth, width)
    ranked = jnp.where(
        jnp.where(alive, rank, -1.0).astype(jnp.int32) == iota((128, moves), 0), 1.0, 0.0
    ).astype(BF16)
    flag_rows = dot_t(jnp.where(peer_is, local, 0.0).astype(BF16), ranked)
    for p in range(lists):
        flag_out[p] = flag_rows[p : p + 1, :]

    pl.semaphore_wait(barrier, lists - 1 + helps - 1)

    def flag_copy(d):
        return pltpu.make_async_remote_copy(
            src_ref=flag_out.at[lax.rem(me + d, lists)],
            dst_ref=flags.at[hp, me],
            send_sem=s_flag.at[d], recv_sem=r_flag.at[d],
            device_id=(lax.rem(me + d, lists), hp), device_id_type=MESH,
        )

    def bucket_copy(d):
        return pltpu.make_async_remote_copy(
            src_ref=buckets.at[lax.rem(me + d, lists)],
            dst_ref=recv.at[me, hp],
            send_sem=s_bkt.at[d], recv_sem=r_bkt.at[d],
            device_id=(lax.rem(me + d, lists), hp), device_id_type=MESH,
        )

    def cent_copy(d):
        return pltpu.make_async_remote_copy(
            src_ref=cents.at[me], dst_ref=cents.at[me],
            send_sem=s_cent.at[d], recv_sem=r_cent.at[d],
            device_id=(lax.rem(me + d, lists), hp), device_id_type=MESH,
        )

    def help_copy(ref, sends, recvs, d):
        return pltpu.make_async_remote_copy(
            src_ref=ref.at[hp], dst_ref=ref.at[hp],
            send_sem=sends.at[d], recv_sem=recvs.at[d],
            device_id=(me, lax.rem(hp + d, helps)), device_id_type=MESH,
        )

    def piece_copy(d, owner_h, target, sends, recvs):
        piece = recv.at[lax.rem(me + lists - d, lists), owner_h]
        return pltpu.make_async_remote_copy(
            src_ref=piece, dst_ref=piece,
            send_sem=sends.at[d], recv_sem=recvs.at[d],
            device_id=(me, target), device_id_type=MESH,
        )

    def to_core(d):
        return piece_copy(d, hp, core, s_core, r_core)

    def to_far(d):
        return piece_copy(d, hp, far, s_y, r_y)

    def relay(d):
        return piece_copy(d, far, core, s_rel, r_rel)

    for d in range(1, helps):
        help_copy(parts, s_part, r_part, d).start()

    def each(lower, upper_, fn):
        def body(d, c):
            fn(d)
            return c

        lax.fori_loop(lower, upper_, body, 0)

    each(1, lists, lambda d: flag_copy(d).start())
    each(1, lists, lambda d: bucket_copy(d).start())
    recv[me, hp] = buckets[me]
    flags[hp, me] = flag_out[me]
    to_core(0).start()
    to_far(0).start()

    for d in range(1, helps):
        help_copy(parts, s_part, r_part, d).wait_recv()
    summed = parts[0]
    for h in range(1, helps):
        summed = summed + parts[h]
    new_c = summed[:, 0:width] / jnp.maximum(summed[:, width : width + 1], 1.0)
    cents[me] = new_c
    each(1, lists, lambda d: cent_copy(d).start())

    each(1, lists, lambda d: flag_copy(d).wait_recv())
    for d in range(1, helps):
        help_copy(flags, s_fgat, r_fgat, d).start()
    for d in range(1, helps):
        help_copy(flags, s_fgat, r_fgat, d).wait_recv()
    for x in range(lists):
        for h in range(helps):
            flag_mat[x * helps + h : x * helps + h + 1, :] = flags[h, x]
    sources = lists * helps
    flag = flag_mat[...]
    before_lane = jnp.where(iota((128, 128), 0) < iota((128, 128), 1), 1.0, 0.0).astype(BF16)
    before_row = jnp.where(
        iota((sources, sources), 0) > iota((sources, sources), 1), 1.0, 0.0
    ).astype(BF16)
    ones = jnp.ones((128, 128), BF16)
    code = jnp.full((sources, 128), -1.0, F32)
    for k in range(list_dev):
        is_k = flag == float(k + 1)
        one_k = jnp.where(is_k, 1.0, 0.0).astype(BF16)
        place = dot(one_k, before_lane) + dot(before_row, dot(one_k, ones).astype(BF16))
        code = jnp.where(is_k, place + float(k * cap), code)
    spread = jnp.where(iota((sources, 128), 1) < depth, code, 0.0)
    step = depth
    while step < 128:
        spread = spread + pltpu.roll(spread, step, 1)
        step *= 2
    lane_h = iota((sources, 128), 1)
    row_h = lax.rem(iota((sources, 128), 0), helps)
    spread = jnp.where((lane_h >= row_h * depth) & (lane_h < (row_h + 1) * depth), spread, 0.0)
    for x in range(lists):
        codes[x] = jnp.sum(spread[x * helps : (x + 1) * helps, :], axis=0, keepdims=True)

    def ready(d):
        @pl.when(d > 0)
        def _():
            bucket_copy(d).wait_recv()
            to_core(d).start()
            to_far(d).start()

    def pass_on(d):
        to_far(d).wait_recv()
        relay(d).start()

    taken = helps * depth

    def place_piece(d, fresh):
        to_core(d).wait_recv()
        relay(d).wait_recv()
        x = lax.rem(me + lists - d, lists)
        put = codes[x][:, 0:taken].astype(jnp.int32)
        onehot = jnp.where(put == iota((list_dev * cap, taken), 0), 1.0, 0.0).astype(BF16)
        a, b = split_parts(recv[x].reshape(taken, width))
        moved = dot(onehot, a) + dot(onehot, b)
        if fresh:
            out[...] = moved.reshape(list_dev, cap, width)
        else:
            out[...] += moved.reshape(list_dev, cap, width)

    def turn(d):
        ready(d)
        pass_on(d - 1)
        place_piece(d - 2, False)

    ready(1)
    pass_on(0)
    ready(2)
    pass_on(1)
    place_piece(0, True)
    each(3, lists, turn)

    each(1, lists, lambda d: cent_copy(d).wait_recv())
    n_c = lists * crows
    table[0:n_c, :] = cents[...].reshape(n_c, width)
    table[n_c:, :] = jnp.zeros((crows, width), F32)
    for k in range(list_dev):
        table[n_c + k : n_c + k + 1, :] = cent[k : k + 1, :]
    every = table[...]
    c_hi, c_lo = split_parts(every)
    cross = dot_t(c_hi, vhi[...]) + dot_t(c_hi, vlo[...]) + dot_t(c_lo, vhi[...])
    score = jnp.sum(every * every, axis=1, keepdims=True) - 2.0 * cross
    c_row = iota((n_c, rows), 0)
    in_block = lax.rem(c_row, crows)
    slot_of = jnp.where(
        in_block < 2 * list_dev,
        lax.div(c_row, crows) * list_dev + lax.div(in_block, 2),
        -1,
    )
    for k in range(list_dev):
        seen = jnp.zeros((n_c, rows), jnp.int32)
        touched = jnp.int32(0)
        for s in range(n_splits):
            at_slot = owner[split_ids[s]]
            hit = jnp.int32(0)
            for n in range(near):
                hit = jnp.maximum(
                    hit, jnp.where(owner[nearby[s, n]] == first + k, 1, 0).astype(jnp.int32)
                )
            touched = jnp.maximum(touched, hit)
            seen = jnp.maximum(seen, jnp.where(slot_of == at_slot, hit, 0))
        block = score[:, k * rows : (k + 1) * rows]
        best = jnp.min(jnp.where(seen > 0, block[0:n_c], 1e30), axis=0, keepdims=True)
        own = block[n_c + k : n_c + k + 1, :]
        top = jnp.where(touched > 0, sizes[k] - hp * rows, 0)
        ok = iota((1, rows), 1) < top
        gains[k : k + 1, :] = jnp.where(ok, (own - best) * (1.0 / width), 0.0)

    pass_on(lists - 1)
    place_piece(lists - 2, False)
    place_piece(lists - 1, False)

    def drain(d):
        flag_copy(d).wait_send()
        bucket_copy(d).wait_send()
        cent_copy(d).wait_send()

    each(1, lists, drain)

    def drain_pieces(d):
        to_core(d).wait_send()
        to_far(d).wait_send()
        relay(d).wait_send()

    each(0, lists, drain_pieces)
    for d in range(1, helps):
        help_copy(parts, s_part, r_part, d).wait_send()
        help_copy(flags, s_fgat, r_fgat, d).wait_send()


def local(
    vectors, labels, list_sizes, centroids, split_ids, nearby, owner_map, mover_source, mover_dest
):
    list_dev, rows, width = vectors.shape
    lists = lax.axis_size("lists")
    helps = lax.axis_size("help")
    moves = mover_source.shape[0]
    most = max(2, (moves + lists - 1) // lists * 2)
    cap = lists * helps * ((most + list_dev - 1) // list_dev)
    depth = (most + 7) // 8 * 8
    crows = (2 * list_dev + 7) // 8 * 8
    vm = pl.BlockSpec(memory_space=pltpu.VMEM)
    sm = pl.BlockSpec(memory_space=pltpu.SMEM)
    sem = pltpu.SemaphoreType.DMA
    gains, arrived = pl.pallas_call(
        functools.partial(kernel, lists, helps, depth, cap, crows),
        out_shape=(
            jax.ShapeDtypeStruct((list_dev, rows), F32),
            jax.ShapeDtypeStruct((list_dev, cap, width), F32),
        ),
        in_specs=[vm] * 5 + [sm] * 4,
        out_specs=(vm, vm),
        scratch_shapes=[
            pltpu.VMEM((list_dev * rows, width), BF16),
            pltpu.VMEM((list_dev * rows, width), BF16),
            pltpu.VMEM((lists, depth, width), F32),
            pltpu.VMEM((lists, helps, depth, width), F32),
            pltpu.VMEM((lists, 1, 128), F32),
            pltpu.VMEM((helps, lists, 1, 128), F32),
            pltpu.VMEM((lists * helps, 128), F32),
            pltpu.VMEM((lists, 1, 128), F32),
            pltpu.VMEM((helps, crows, width + 128), F32),
            pltpu.VMEM((lists, crows, width), F32),
            pltpu.VMEM((lists * crows + crows, width), F32),
            sem((lists,)), sem((lists,)), sem((helps,)), sem((helps,)),
            sem((lists,)), sem((lists,)), sem((lists,)), sem((lists,)),
            sem((lists,)), sem((lists,)), sem((lists,)), sem((lists,)),
            sem((helps,)), sem((helps,)), sem((lists,)), sem((lists,)),
        ],
        compiler_params=pltpu.CompilerParams(
            collective_id=0, has_side_effects=True, vmem_limit_bytes=56 * 1024 * 1024
        ),
    )(
        vectors, labels, centroids, mover_source.reshape(1, moves), mover_dest.reshape(1, moves),
        list_sizes, split_ids, nearby, owner_map,
    )
    return gains, arrived


def solution(mesh):
    in_specs = (
        P("lists", "help", None),
        P("lists", "help"),
        P("lists"),
        P("lists", None),
        P(),
        P(),
        P(),
        P(("lists", "help")),
        P(("lists", "help")),
    )
    out_specs = (P("lists", "help"), P("lists", None, None))
    return jax.shard_map(local, mesh=mesh, in_specs=in_specs, out_specs=out_specs, check_vma=False)
```

time: 168 us -> 51.6 us (0.31)
  blocking collectives: 114 us -> 0 us
  Pallas kernels: 0 us -> 45.8 us
  other arithmetic: 15.3 us -> 0 us
  between operations: 14.2 us -> 0.64 us
  local copies, waits for them, and re-layouts: 16.7 us -> 5 us
  matrix products: 3.97 us -> 0 us
  starting transfers between devices: 3.63 us -> 0 us
    pallas_call x0 -> x1, Pallas kernels: none -> 45.8 us  [local(): pl.pallas_call(functools.partial(kernel, lists, helps, depth, cap, crows)...]
    unnamed x1 -> x0, blocking collectives: 42 us -> none
    psum x1 -> x0, blocking collectives: 41.4 us -> none  [local(): lax.psum((jnp.einsum('sk,kad->sad', select, partial_value, precision=HIGH...]
    all_to_all x1 -> x0, blocking collectives: 24.8 us -> none  [local(): lax.all_to_all(buckets.reshape(lists_count, depth, width), 'lists', split...]
    select_n x7 -> x0, other arithmetic: 12.7 us -> none  [the longest x1 10.7 us: local(): dest_dev = dest_slot // list_dev]
    scatter x3 -> x0, local copies, waits for them, and re-layouts: 11.2 us -> none  [the longest x1 7.46 us: place_rows(): jnp.zeros((slots_total, width), jnp.float32).at[where_to]]
    all_gather x1 -> x0, blocking collectives: 5.32 us -> none  [local(): lax.all_gather(landed_codes.reshape(-1), 'help', axis=0, tiled=True)]
    unnamed x17 -> x2, local copies, waits for them, and re-layouts: 0.36 us -> 5 us
  transfers between devices with their start and end apart: 2 -> 0, of which waited for: 0 -> 0; matrix products, arithmetic and copies ran while one was open for 6% -> 0% of each run, Pallas kernels for 0% -> 0%
where the time goes in v1:
time: 51.6 us; the launch traced here: 51.4 us
  Pallas kernels  45.8 us (89%)
  local copies, waits for them, and re-layouts  5 us (10%)
  between operations  0.64 us (1%)
    pallas_call x1, Pallas kernels, local(): pl.pallas_call(functools.partial(kernel, lists, helps, depth, cap, crows)...  45.8 us
    unnamed x2, local copies, waits for them, and re-layouts  5 us

profile of v1, /device:TPU:0, one launch (start us, length us, event | category | flops | bytes accessed | tf_op | source)
XLA Modules:
  0.0 51.4 jit_solution(11736933213819144214)
XLA Ops:
  0.6 45.8 %shard_map.104 = (f32[2,256]{1,0:T(2,128)}, f32[2,512,768]{2,1,0:T(8,128)}) custom-call(f32[2,256,768]{2,1,0:T(8,128)} %vec.1, s32[2,256]{1,0:T(2,128)} %labels.1, f32[2,768]{1,0:T(2,128)} %cent.1, s32[1,128]{1,0:T(1,128)} %bitcast.2, s32[1,128]{1,0:T(1,128)} %bitcast.3, s32[2]{0:T(128)} %sizes.1, s32[4]{0:T(128)} %split_ids.1, s32[4,8]{1,0:T(4,128)} %nearby.1, ...), custom_call_target="tpu_custom_call" | custom-call | tf_op jit(solution)/shard_map/pallas_call | solution.py:331
  46.4 1.2 %copy.13 = f32[2,256]{1,0:T(2,128)} copy(f32[2,256]{1,0:T(2,128)} %get-tuple-element.4) | data formatting | bytes 4096
  47.7 3.8 %copy.14 = f32[2,512,768]{2,1,0:T(8,128)} copy(f32[2,512,768]{2,1,0:T(8,128)} %get-tuple-element.5) | data formatting | bytes 6291456

commit v2 on v1

--- a/solution.py
+++ b/solution.py
@@ -66,26 +66,6 @@
     hi, lo = split_parts(vec[...].reshape(n_rows, width))
     vhi[...] = hi
     vlo[...] = lo
-
-    lane = iota((crows, n_rows), 1)
-    row = iota((crows, n_rows), 0)
-    label = jnp.concatenate([labels[k : k + 1, :] for k in range(list_dev)], axis=1)
-    limit = jnp.zeros((1, n_rows), jnp.int32)
-    lane1 = iota((1, n_rows), 1)
-    for k in range(list_dev):
-        inside = (lane1 >= k * rows) & (lane1 < (k + 1) * rows)
-        limit = jnp.where(inside, sizes[k] + k * rows - hp * rows, limit)
-    live_label = jnp.where(lane1 < limit, label, -1)
-    half = jnp.zeros((crows, n_rows), F32)
-    for k in range(list_dev):
-        for a in range(2):
-            pick = (row == 2 * k + a) & (lane >= k * rows) & (lane < (k + 1) * rows)
-            half = jnp.where(pick & (live_label == a), 1.0, half)
-    hb = half.astype(BF16)
-    mine = dot(hb, hi) + dot(hb, lo)
-    number = jnp.sum(half, axis=1, keepdims=True)
-    parts[hp, :, 0:width] = mine
-    parts[hp, :, width:] = jnp.broadcast_to(number, (crows, 128))
 
     dest = mdst[...]
     slot = jnp.full((1, moves), -1, jnp.int32)
@@ -160,9 +140,6 @@
     def relay(d):
         return piece_copy(d, far, core, s_rel, r_rel)
 
-    for d in range(1, helps):
-        help_copy(parts, s_part, r_part, d).start()
-
     def each(lower, upper_, fn):
         def body(d, c):
             fn(d)
@@ -176,6 +153,29 @@
     flags[hp, me] = flag_out[me]
     to_core(0).start()
     to_far(0).start()
+
+    lane = iota((crows, n_rows), 1)
+    row = iota((crows, n_rows), 0)
+    label = jnp.concatenate([labels[k : k + 1, :] for k in range(list_dev)], axis=1)
+    limit = jnp.zeros((1, n_rows), jnp.int32)
+    lane1 = iota((1, n_rows), 1)
+    for k in range(list_dev):
+        inside = (lane1 >= k * rows) & (lane1 < (k + 1) * rows)
+        limit = jnp.where(inside, sizes[k] + k * rows - hp * rows, limit)
+    live_label = jnp.where(lane1 < limit, label, -1)
+    half = jnp.zeros((crows, n_rows), F32)
+    for k in range(list_dev):
+        for a in range(2):
+            pick = (row == 2 * k + a) & (lane >= k * rows) & (lane < (k + 1) * rows)
+            half = jnp.where(pick & (live_label == a), 1.0, half)
+    hb = half.astype(BF16)
+    mine = dot(hb, hi) + dot(hb, lo)
+    number = jnp.sum(half, axis=1, keepdims=True)
+    parts[hp, :, 0:width] = mine
+    parts[hp, :, width:] = jnp.broadcast_to(number, (crows, 128))
+
+    for d in range(1, helps):
+        help_copy(parts, s_part, r_part, d).start()
 
     for d in range(1, helps):
         help_copy(parts, s_part, r_part, d).wait_recv()
@@ -314,6 +314,15 @@
         help_copy(flags, s_fgat, r_fgat, d).wait_send()
 
 
+def write_out(gains, arrived, gains_to, arrived_to, sems):
+    rows = pltpu.make_async_copy(arrived, arrived_to, sems.at[0])
+    few = pltpu.make_async_copy(gains, gains_to, sems.at[1])
+    rows.start()
+    few.start()
+    few.wait()
+    rows.wait()
+
+
 def local(
     vectors, labels, list_sizes, centroids, split_ids, nearby, owner_map, mover_source, mover_dest
 ):
@@ -331,8 +340,8 @@
     gains, arrived = pl.pallas_call(
         functools.partial(kernel, lists, helps, depth, cap, crows),
         out_shape=(
-            jax.ShapeDtypeStruct((list_dev, rows), F32),
-            jax.ShapeDtypeStruct((list_dev, cap, width), F32),
+            pltpu.VMEM((list_dev, rows), F32),
+            pltpu.VMEM((list_dev, cap, width), F32),
         ),
         in_specs=[vm] * 5 + [sm] * 4,
         out_specs=(vm, vm),
@@ -360,7 +369,18 @@
         vectors, labels, centroids, mover_source.reshape(1, moves), mover_dest.reshape(1, moves),
         list_sizes, split_ids, nearby, owner_map,
     )
-    return gains, arrived
+    hbm = pl.BlockSpec(memory_space=pl.ANY)
+    return pl.pallas_call(
+        write_out,
+        out_shape=(
+            jax.ShapeDtypeStruct((list_dev, rows), F32),
+            jax.ShapeDtypeStruct((list_dev, cap, width), F32),
+        ),
+        in_specs=[vm, vm],
+        out_specs=(hbm, hbm),
+        scratch_shapes=[sem((2,))],
+        compiler_params=pltpu.CompilerParams(vmem_limit_bytes=8 * 1024 * 1024),
+    )(gains, arrived)
 
 
 def solution(mesh):

time: 51.6 us -> 46.4 us (0.90)
  local copies, waits for them, and re-layouts: 5 us -> 0 us
    unnamed x2 -> x0, local copies, waits for them, and re-layouts: 5 us -> none
    pallas_call x1, Pallas kernels: 45.8 us -> 44 us  [local(): pl.pallas_call(functools.partial(kernel, lists, helps, depth, cap, crows)...]
    pallas_call x0 -> x1, Pallas kernels: none -> 1.68 us  [local(): pl.pallas_call(write_out, out_shape=(jax.ShapeDtypeStruct((list_dev, rows...]
where the time goes in v2:
time: 46.4 us; the launch traced here: 46.3 us
  Pallas kernels  45.6 us (98%)
  between operations  0.64 us (1%)
    pallas_call x1, Pallas kernels, local(): pl.pallas_call(functools.partial(kernel, lists, helps, depth, cap, crows)...  44 us
    pallas_call x1, Pallas kernels, local(): pl.pallas_call(write_out, out_shape=(jax.ShapeDtypeStruct((list_dev, rows...  1.68 us

profile of v2, /device:TPU:0, one launch (start us, length us, event | category | flops | bytes accessed | tf_op | source)
XLA Modules:
  0.0 46.3 jit_solution(14456561759022613577)
XLA Ops:
  0.6 44.0 %shard_map.104 = (f32[2,256]{1,0:T(2,128)S(1)}, f32[2,512,768]{2,1,0:T(8,128)S(1)}) custom-call(f32[2,256,768]{2,1,0:T(8,128)} %vec.1, s32[2,256]{1,0:T(2,128)} %labels.1, f32[2,768]{1,0:T(2,128)} %cent.1, s32[1,128]{1,0:T(1,128)} %bitcast.2, s32[1,128]{1,0:T(1,128)} %bitcast.3, s32[2]{0:T(128)} %sizes.1, s32[4]{0:T(128)} %split_ids.1, s32[4,8]{1,0:T(4,128)} %nearby.1, ...), custom_call_target="tpu_custom_call" | custom-call | tf_op jit(solution)/shard_map/pallas_call | solution.py:340
  44.6 1.7 %shard_map.105 = (f32[2,256]{1,0:T(2,128)}, f32[2,512,768]{2,1,0:T(8,128)}) custom-call(f32[2,256]{1,0:T(2,128)S(1)} %get-tuple-element.4.gains, f32[2,512,768]{2,1,0:T(8,128)S(1)} %get-tuple-element.5.arrived), custom_call_target="tpu_custom_call" | custom-call | tf_op jit(solution)/shard_map/pallas_call | solution.py:373

commit v3 on v2

--- a/solution.py
+++ b/solution.py
@@ -93,6 +93,13 @@
 
     pl.semaphore_wait(barrier, lists - 1 + helps - 1)
 
+    def hop(k):
+        k = jnp.int32(k)
+        j = k - 1
+        turn_ = 1 - 2 * lax.rem(j + 2, 2)
+        away = lists // 2 + turn_ * lax.div(j + 1, 2)
+        return away * jnp.minimum(k, 1)
+
     def flag_copy(d):
         return pltpu.make_async_remote_copy(
             src_ref=flag_out.at[lax.rem(me + d, lists)],
@@ -103,10 +110,10 @@
 
     def bucket_copy(d):
         return pltpu.make_async_remote_copy(
-            src_ref=buckets.at[lax.rem(me + d, lists)],
+            src_ref=buckets.at[lax.rem(me + hop(d), lists)],
             dst_ref=recv.at[me, hp],
             send_sem=s_bkt.at[d], recv_sem=r_bkt.at[d],
-            device_id=(lax.rem(me + d, lists), hp), device_id_type=MESH,
+            device_id=(lax.rem(me + hop(d), lists), hp), device_id_type=MESH,
         )
 
     def cent_copy(d):
@@ -124,7 +131,7 @@
         )
 
     def piece_copy(d, owner_h, target, sends, recvs):
-        piece = recv.at[lax.rem(me + lists - d, lists), owner_h]
+        piece = recv.at[lax.rem(me + lists - hop(d), lists), owner_h]
         return pltpu.make_async_remote_copy(
             src_ref=piece, dst_ref=piece,
             send_sem=sends.at[d], recv_sem=recvs.at[d],
@@ -234,7 +241,7 @@
     def place_piece(d, fresh):
         to_core(d).wait_recv()
         relay(d).wait_recv()
-        x = lax.rem(me + lists - d, lists)
+        x = lax.rem(me + lists - hop(d), lists)
         put = codes[x][:, 0:taken].astype(jnp.int32)
         onehot = jnp.where(put == iota((list_dev * cap, taken), 0), 1.0, 0.0).astype(BF16)
         a, b = split_parts(recv[x].reshape(taken, width))

time: 46.4 us -> 46.3 us (level)
  no operation moved by 1% of the time
where the time goes in v3:
time: 46.3 us; the launch traced here: 46.2 us
  Pallas kernels  45.5 us (98%)
  between operations  0.64 us (1%)
    pallas_call x1, Pallas kernels, local(): pl.pallas_call(functools.partial(kernel, lists, helps, depth, cap, crows)...  43.9 us
    pallas_call x1, Pallas kernels, local(): pl.pallas_call(write_out, out_shape=(jax.ShapeDtypeStruct((list_dev, rows...  1.68 us

profile of v3, /device:TPU:0, one launch (start us, length us, event | category | flops | bytes accessed | tf_op | source)
XLA Modules:
  0.0 46.2 jit_solution(7241075940343546398)
XLA Ops:
  0.6 43.9 %shard_map.104 = (f32[2,256]{1,0:T(2,128)S(1)}, f32[2,512,768]{2,1,0:T(8,128)S(1)}) custom-call(f32[2,256,768]{2,1,0:T(8,128)} %vec.1, s32[2,256]{1,0:T(2,128)} %labels.1, f32[2,768]{1,0:T(2,128)} %cent.1, s32[1,128]{1,0:T(1,128)} %bitcast.2, s32[1,128]{1,0:T(1,128)} %bitcast.3, s32[2]{0:T(128)} %sizes.1, s32[4]{0:T(128)} %split_ids.1, s32[4,8]{1,0:T(4,128)} %nearby.1, ...), custom_call_target="tpu_custom_call" | custom-call | tf_op jit(solution)/shard_map/pallas_call | solution.py:347
  44.5 1.7 %shard_map.105 = (f32[2,256]{1,0:T(2,128)}, f32[2,512,768]{2,1,0:T(8,128)}) custom-call(f32[2,256]{1,0:T(2,128)S(1)} %get-tuple-element.4.gains, f32[2,512,768]{2,1,0:T(8,128)S(1)} %get-tuple-element.5.arrived), custom_call_target="tpu_custom_call" | custom-call | tf_op jit(solution)/shard_map/pallas_call | solution.py:380

commit v4 on v3

--- a/solution.py
+++ b/solution.py
@@ -245,7 +245,12 @@
         put = codes[x][:, 0:taken].astype(jnp.int32)
         onehot = jnp.where(put == iota((list_dev * cap, taken), 0), 1.0, 0.0).astype(BF16)
         a, b = split_parts(recv[x].reshape(taken, width))
-        moved = dot(onehot, a) + dot(onehot, b)
+        if taken % 128 == 0:
+            moved = dot(
+                jnp.concatenate([onehot, onehot], axis=1), jnp.concatenate([a, b], axis=0)
+            )
+        else:
+            moved = dot(onehot, a) + dot(onehot, b)
         if fresh:
             out[...] = moved.reshape(list_dev, cap, width)
         else:

time: 46.3 us -> 44.1 us (0.952)
  Pallas kernels: 45.5 us -> 43.1 us
    pallas_call x1, Pallas kernels: 43.9 us -> 41.4 us  [local(): pl.pallas_call(functools.partial(kernel, lists, helps, depth, cap, crows)...]
where the time goes in v4:
time: 44.1 us; the launch traced here: 43.7 us
  Pallas kernels  43.1 us (98%)
  between operations  0.64 us (1%)
    pallas_call x1, Pallas kernels, local(): pl.pallas_call(functools.partial(kernel, lists, helps, depth, cap, crows)...  41.4 us
    pallas_call x1, Pallas kernels, local(): pl.pallas_call(write_out, out_shape=(jax.ShapeDtypeStruct((list_dev, rows...  1.68 us

profile of v4, /device:TPU:0, one launch (start us, length us, event | category | flops | bytes accessed | tf_op | source)
XLA Modules:
  0.0 43.7 jit_solution(1652924032339275323)
XLA Ops:
  0.6 41.4 %shard_map.104 = (f32[2,256]{1,0:T(2,128)S(1)}, f32[2,512,768]{2,1,0:T(8,128)S(1)}) custom-call(f32[2,256,768]{2,1,0:T(8,128)} %vec.1, s32[2,256]{1,0:T(2,128)} %labels.1, f32[2,768]{1,0:T(2,128)} %cent.1, s32[1,128]{1,0:T(1,128)} %bitcast.2, s32[1,128]{1,0:T(1,128)} %bitcast.3, s32[2]{0:T(128)} %sizes.1, s32[4]{0:T(128)} %split_ids.1, s32[4,8]{1,0:T(4,128)} %nearby.1, ...), custom_call_target="tpu_custom_call" | custom-call | tf_op jit(solution)/shard_map/pallas_call | solution.py:352
  42.0 1.7 %shard_map.105 = (f32[2,256]{1,0:T(2,128)}, f32[2,512,768]{2,1,0:T(8,128)}) custom-call(f32[2,256]{1,0:T(2,128)S(1)} %get-tuple-element.4.gains, f32[2,512,768]{2,1,0:T(8,128)S(1)} %get-tuple-element.5.arrived), custom_call_target="tpu_custom_call" | custom-call | tf_op jit(solution)/shard_map/pallas_call | solution.py:385

commit v5 on v3

--- a/solution.py
+++ b/solution.py
@@ -238,30 +238,42 @@
 
     taken = helps * depth
 
-    def place_piece(d, fresh):
-        to_core(d).wait_recv()
-        relay(d).wait_recv()
-        x = lax.rem(me + lists - hop(d), lists)
-        put = codes[x][:, 0:taken].astype(jnp.int32)
-        onehot = jnp.where(put == iota((list_dev * cap, taken), 0), 1.0, 0.0).astype(BF16)
-        a, b = split_parts(recv[x].reshape(taken, width))
-        moved = dot(onehot, a) + dot(onehot, b)
+    def place_pieces(steps, fresh):
+        hots, terms = [], []
+        for d in steps:
+            to_core(d).wait_recv()
+            relay(d).wait_recv()
+            x = lax.rem(me + lists - hop(d), lists)
+            put = codes[x][:, 0:taken].astype(jnp.int32)
+            onehot = jnp.where(put == iota((list_dev * cap, taken), 0), 1.0, 0.0).astype(BF16)
+            hots += [onehot, onehot]
+            terms += split_parts(recv[x].reshape(taken, width))
+        if taken % 128 == 0:
+            moved = dot(jnp.concatenate(hots, axis=1), jnp.concatenate(terms, axis=0))
+        else:
+            moved = sum(dot(p, t) for p, t in zip(hots, terms))
         if fresh:
             out[...] = moved.reshape(list_dev, cap, width)
         else:
             out[...] += moved.reshape(list_dev, cap, width)
 
-    def turn(d):
+    def turn(t):
+        d = 2 * t + 1
         ready(d)
         pass_on(d - 1)
-        place_piece(d - 2, False)
+        ready(d + 1)
+        pass_on(d)
+        place_pieces((d - 1, d), False)
 
     ready(1)
     pass_on(0)
     ready(2)
     pass_on(1)
-    place_piece(0, True)
-    each(3, lists, turn)
+    place_pieces((0, 1), True)
+    each(1, lists // 2 - 1, turn)
+    ready(lists - 1)
+    pass_on(lists - 2)
+    pass_on(lists - 1)
 
     each(1, lists, lambda d: cent_copy(d).wait_recv())
     n_c = lists * crows
@@ -299,9 +311,7 @@
         ok = iota((1, rows), 1) < top
         gains[k : k + 1, :] = jnp.where(ok, (own - best) * (1.0 / width), 0.0)
 
-    pass_on(lists - 1)
-    place_piece(lists - 2, False)
-    place_piece(lists - 1, False)
+    place_pieces((lists - 2, lists - 1), False)
 
     def drain(d):
         flag_copy(d).wait_send()

time: 46.3 us -> 48.4 us (1.045)
  Pallas kernels: 45.5 us -> 47.7 us
    pallas_call x1, Pallas kernels: 43.9 us -> 46 us  [local(): pl.pallas_call(functools.partial(kernel, lists, helps, depth, cap, crows)...]
where the time goes in v5:
time: 48.4 us; the launch traced here: 48.3 us
  Pallas kernels  47.7 us (99%)
  between operations  0.64 us (1%)
    pallas_call x1, Pallas kernels, local(): pl.pallas_call(functools.partial(kernel, lists, helps, depth, cap, crows)...  46 us
    pallas_call x1, Pallas kernels, local(): pl.pallas_call(write_out, out_shape=(jax.ShapeDtypeStruct((list_dev, rows...  1.68 us

profile of v5, /device:TPU:0, one launch (start us, length us, event | category | flops | bytes accessed | tf_op | source)
XLA Modules:
  0.0 48.3 jit_solution(1265088056830926299)
XLA Ops:
  0.6 46.0 %shard_map.104 = (f32[2,256]{1,0:T(2,128)S(1)}, f32[2,512,768]{2,1,0:T(8,128)S(1)}) custom-call(f32[2,256,768]{2,1,0:T(8,128)} %vec.1, s32[2,256]{1,0:T(2,128)} %labels.1, f32[2,768]{1,0:T(2,128)} %cent.1, s32[1,128]{1,0:T(1,128)} %bitcast.2, s32[1,128]{1,0:T(1,128)} %bitcast.3, s32[2]{0:T(128)} %sizes.1, s32[4]{0:T(128)} %split_ids.1, s32[4,8]{1,0:T(4,128)} %nearby.1, ...), custom_call_target="tpu_custom_call" | custom-call | tf_op jit(solution)/shard_map/pallas_call | solution.py:357
  46.6 1.7 %shard_map.105 = (f32[2,256]{1,0:T(2,128)}, f32[2,512,768]{2,1,0:T(8,128)}) custom-call(f32[2,256]{1,0:T(2,128)S(1)} %get-tuple-element.4.gains, f32[2,512,768]{2,1,0:T(8,128)S(1)} %get-tuple-element.5.arrived), custom_call_target="tpu_custom_call" | custom-call | tf_op jit(solution)/shard_map/pallas_call | solution.py:390
